TPU v7x, 32 devices: a whole 2x2x4 slice. The times are simulated.
32 devices in a mesh: groups: 2 (over x), pool: 16 (over z, y, core).
Axes of the slice: x: 2, y: 2, z: 4, core: 2. Of those that a mesh axis runs over, the one named last changes fastest.
Arguments:
- queries: bfloat16 [8192, 4096], P(('groups', 'pool')), parts along dimension 0, may hold values from -180 to 180
- new_kv: bfloat16 [8192, 1024], P(('groups', 'pool')), parts along dimension 0, may hold values from -6 to 6
- prefix_store: bfloat16 [2048, 8, 1024], P(('groups', 'pool')), parts along dimension 0, may hold values from -6 to 6
- page_owner: int32 [32, 16], P('groups'), parts along dimension 0, may hold values from 0 to 15, each once within a row
- page_slot: int32 [32, 16], P('groups'), parts along dimension 0, may hold values from 0 to 63
- prefix_pages: int32 [32], P('groups'), parts along dimension 0, may hold values from 1 to 16, 128 in all
- decode_dest: int32 [32, 32], P(('groups', 'pool')), parts along dimension 0, may hold values from 0 to 15, as said below
Outputs:
- attention: bfloat16 [8192, 4096], P(('groups', 'pool')), parts along dimension 0
- decode_inbox: bfloat16 [1024, 8, 1024], P(('groups', 'pool')), parts along dimension 0
There are 2 independent parts, one for each index of `groups`. A program takes and returns all parts, laid end to end along the dimension named above; each array names one. Nothing has to cross between parts.
Inputs may be any that keep to these rules, and one draw needn't show every extreme that they name: `page_owner`: each row names every device of the pool once. `prefix_pages`: the entries sum to 128; the largest is 16. `decode_dest`: a device sends at most 2 of its 32 new pages to one decode owner; one decode owner receives exactly 2 from every device.
All inputs are finite; a program needn't handle non-finite values.
Results may differ from a plain program's by a relative error of at most 0.0027.
Values may be sent and summed in bfloat16 or wider, within the bound.
A program may use at most 128 MiB of HBM per device.

v0:
```python
import math

import jax
import jax.numpy as jnp
from jax import lax
from jax.sharding import PartitionSpec as P

H = 32
KVH = 4
HD = 128
PAGE = 8


masked_score = -1e30
block_keys = 256


def empty_running(query_groups):
    tokens, kv_heads, group_size, head_dim = query_groups.shape
    shape_rows = (kv_heads, group_size, tokens)
    return (
        jnp.full(shape_rows, masked_score, jnp.float32),
        jnp.zeros(shape_rows, jnp.float32),
        jnp.zeros(shape_rows + (head_dim,), jnp.float32),
    )


def absorb_block(running, query_groups, kv_block, key_valid):
    run_max, run_total, run_acc = running
    kv_heads = query_groups.shape[1]
    head_dim = query_groups.shape[3]
    key_count = kv_block.shape[0]
    width_keys = kv_heads * head_dim
    key_rows = kv_block[:, :width_keys].reshape(key_count, kv_heads, head_dim)
    value_rows = kv_block[:, width_keys:].reshape(key_count, kv_heads, head_dim)
    scores = jnp.einsum(
        "tkgd,skd->kgts", query_groups, key_rows, preferred_element_type=jnp.float32
    ) * (1.0 / math.sqrt(head_dim))
    scores = jnp.where(key_valid, scores, masked_score)
    new_max = jnp.maximum(run_max, jnp.max(scores, axis=-1))
    factor = jnp.exp(run_max - new_max)
    weights = jnp.where(key_valid, jnp.exp(scores - new_max[..., None]), 0.0)
    run_total = factor * run_total + jnp.sum(weights, axis=-1)
    mixed_heads = jnp.einsum(
        "kgts,skd->kgtd",
        weights.astype(jnp.bfloat16),
        value_rows,
        preferred_element_type=jnp.float32,
    )
    return (new_max, run_total, factor[..., None] * run_acc + mixed_heads)


def attend_pages(running, query_groups, ordered, count_pages):
    per_block = max(1, block_keys // PAGE)
    total_pages = ordered.shape[0] // PAGE
    padded_pages = (total_pages + per_block - 1) // per_block * per_block
    if padded_pages > total_pages:
        ordered = jnp.pad(ordered, ((0, (padded_pages - total_pages) * PAGE), (0, 0)))
    block_rows = per_block * PAGE
    block_count = (count_pages + per_block - 1) // per_block

    def one_block(block_index, carried):
        kv_block = lax.dynamic_slice_in_dim(ordered, block_index * block_rows, block_rows, 0)
        key_page = (block_index * block_rows + jnp.arange(block_rows, dtype=jnp.int32)) // PAGE
        return absorb_block(carried, query_groups, kv_block, (key_page < count_pages)[None, :])

    return lax.fori_loop(0, block_count, one_block, running)


def self_attend(query_groups, own_rows):
    tokens = own_rows.shape[0]
    positions = jnp.arange(tokens, dtype=jnp.int32)
    running = empty_running(query_groups)
    key_valid = (0 + positions)[None, :] <= positions[:, None]
    running = absorb_block(running, query_groups, own_rows, key_valid)
    return running


def finish(running):
    mixed_heads = running[2] / running[1][..., None]
    kv_heads, group_size, tokens, head_dim = mixed_heads.shape
    return (
        jnp.transpose(mixed_heads, (2, 0, 1, 3))
        .reshape(tokens, kv_heads * group_size * head_dim)
        .astype(jnp.bfloat16)
    )


def build_outbox(new_kv, dest_row, pool_size):
    page_count = dest_row.shape[0]
    kv_width = new_kv.shape[1]
    slots_each = max(1, (page_count + pool_size - 1) // pool_size)
    order_ids = jnp.arange(page_count, dtype=jnp.int32)
    same_owner = dest_row[:, None] == dest_row[None, :]
    earlier = order_ids[None, :] < order_ids[:, None]
    rank_in_owner = jnp.sum(same_owner & earlier, axis=1)
    target_slot = dest_row * slots_each + rank_in_owner
    slot_ids = jnp.arange(pool_size * slots_each, dtype=jnp.int32)
    match_slot = target_slot[None, :] == slot_ids[:, None]
    source_page = jnp.sum(jnp.where(match_slot, order_ids[None, :], 0), axis=1)
    filled = jnp.any(match_slot, axis=1)
    page_data = new_kv.reshape(page_count, PAGE, kv_width)[source_page]
    outgoing = jnp.where(filled[:, None, None], page_data, jnp.zeros_like(page_data))
    return outgoing.reshape(pool_size, slots_each, PAGE, kv_width)


def on_device(queries, new_kv, prefix_store, page_owner, page_slot, prefix_pages, decode_dest):
    pool_size = lax.axis_size("pool")
    myself = lax.axis_index("pool")
    tokens = queries.shape[0]
    kv_width = new_kv.shape[1]
    query_groups = queries.reshape(tokens, KVH, H // KVH, HD)
    columns = jnp.arange(pool_size, dtype=jnp.int32)
    owner_match = page_owner == myself
    row_of = jnp.sum(jnp.where(owner_match, columns[None, :], 0), axis=1)
    slot_of = jnp.sum(jnp.where(owner_match, page_slot, 0), axis=1)
    my_owners = page_owner[myself]
    stored = prefix_store[slot_of]
    prefix_out = jnp.where((row_of < prefix_pages)[:, None, None], stored, jnp.zeros_like(stored))
    outbox = build_outbox(new_kv, decode_dest[0], pool_size)
    slots_each = outbox.shape[1]
    running = self_attend(query_groups, new_kv)
    incoming = lax.all_to_all(outbox, "pool", split_axis=0, concat_axis=0, tiled=True)
    arrived = lax.all_to_all(prefix_out, "pool", split_axis=0, concat_axis=0, tiled=True)
    decode_inbox = incoming.reshape(pool_size * slots_each, PAGE, kv_width)
    ordered = arrived[my_owners].reshape(pool_size * PAGE, kv_width)
    running = attend_pages(running, query_groups, ordered, prefix_pages[myself])
    attention = finish(running)
    return (attention, decode_inbox)


def solution(mesh):
    return jax.shard_map(
        on_device,
        mesh=mesh,
        in_specs=(
            P(("groups", "pool"), None),
            P(("groups", "pool"), None),
            P(("groups", "pool"), None, None),
            P("groups", None),
            P("groups", None),
            P("groups"),
            P(("groups", "pool"), None),
        ),
        out_specs=(P(("groups", "pool"), None), P(("groups", "pool"), None, None)),
        check_vma=False,
    )
```

profile of v0, /device:TPU:0, one launch (start us, length us, event | category | flops | bytes accessed | tf_op | source)
XLA Modules:
  0.0 75.2 jit_solution(8457165797203795155)
XLA Ops:
  3.9 7.4 %all-to-all-start = ((bf16[16,8,1024]{2,1,0:T(8,128)(2,1)}), bf16[16,8,1024]{2,1,0:T(8,128)(2,1)}, u32[]{:S(2)}, u32[]{:S(2)}) async-start(bf16[16,8,1024]{2,1,0:T(8,128)(2,1)} %broadcast_select_fusion.1), calls=%async_computation | async-start | bytes 524288 | tf_op jit(solution)/shard_map/all_to_all | solution.py:124
  13.2 3.3 %copy.42 = bf16[256,4096]{0,1:T(8,128)(2,1)S(1)} copy(bf16[256,4096]{1,0:T(8,128)(2,1)} %param.9) | data formatting | bytes 4194304 | tf_op args[0]
  16.5 2.2 %fusion.42 = (bf16[256,512]{1,0:T(8,128)(2,1)}, bf16[256,512]{1,0:T(8,128)(2,1)}) fusion(bf16[256,1024]{1,0:T(8,128)(2,1)} %param.10), kind=kLoop, calls=%fused_computation.73 | loop fusion | bytes 1048576 | tf_op jit(solution)/shard_map/slice | solution.py:35
  18.7 1.1 %copy.66 = bf16[256,512]{0,1:T(8,128)(2,1)S(1)} copy(bf16[256,512]{1,0:T(8,128)(2,1)} %get-tuple-element.159) | data formatting | bytes 524288
  19.8 1.5 %fusion.18 = (f32[4,8,256]{2,1,0:T(8,128)S(1)}, f32[4,256,256,8]{2,1,3,0:T(8,128)S(1)}) fusion(pred[256,256]{0,1:T(8,128)(4,1)S(1)} %iota_compare_fusion, bf16[256,4,128,1]{0,2,3,1:T(8,128)(2,1)S(1)} %bitcast.109, bf16[256,4,8,128]{0,3,2,1:T(8,128)(2,1)S(1)} %bitcast.102), kind=kOutput, calls=%fused_computation.30 | convolution fusion | flops 543154176 | bytes 10846208 | tf_op jit(solution)/shard_map/tkgd,skd->kgts/dot_general | solution.py:36
  21.3 3.2 %copy-done.1 = f32[4,256,256,8]{2,1,3,0:T(8,128)} copy-done((f32[4,256,256,8]{2,1,3,0:T(8,128)}, f32[4,256,256,8]{2,1,3,0:T(8,128)S(1)}, u32[]{:S(2)}) %copy-start.1) | copy-done | bytes 8388632
  24.5 2.1 %fusion.20 = f32[4,8,256]{2,1,0:T(8,128)S(1)} fusion(f32[4,256,256,8]{2,1,3,0:T(8,128)S(1)} %get-tuple-element.163, f32[4,8,256]{2,1,0:T(8,128)S(1)} %broadcast_maximum_fusion, pred[256,256]{0,1:T(8,128)(4,1)S(1)} %iota_compare_fusion), kind=kLoop, calls=%fused_computation.32 | loop fusion | flops 10477568 | bytes 8519680 | tf_op jit(solution)/shard_map/reduce_sum | solution.py:43
  27.4 7.0 %broadcast_add_fusion = f32[4,8,256,128]{3,2,1,0:T(8,128)} fusion(f32[4,8,256]{2,1,0:T(8,128)} %get-tuple-element.160, bf16[256,4,128,1]{0,2,3,1:T(8,128)(2,1)S(1)} %bitcast.111, f32[4,256,256,8]{2,1,3,0:T(8,128)} %copy-done.1, f32[4,8,256]{2,1,0:T(8,128)S(1)} %broadcast_maximum_fusion, pred[256,256]{0,1:T(8,128)(4,1)S(1)} %iota_compare_fusion), kind=kOutput, calls=%fused_computation.41 | convolution fusion | flops 548405248 | bytes 12976128 | tf_op jit(solution)/shard_map/kgts,skd->kgtd/dot_general | solution.py:44
  35.8 3.0 %copy.49 = bf16[256,4,8,128]{3,0,2,1:T(8,128)(2,1)S(1)} copy(bf16[256,4,8,128]{0,3,2,1:T(8,128)(2,1)} %bitcast.103) | data formatting | bytes 4194304 | tf_op jit(solution)/shard_map/while | solution.py:67
  39.0 2.4 %gather_fusion.2 = bf16[32,8,1024]{2,1,0:T(8,128)(2,1)} fusion(bf16[32,8,1024]{2,1,0:T(8,128)(2,1)} %bitcast.107, s32[1024]{0:T(1024)S(1)} %pad_clamp_fusion), kind=kCustom, calls=%fused_computation.2 | custom fusion | bytes 1048704 | tf_op jit(solution)/shard_map/gather | solution.py:102
  42.1 1.9 %broadcast_select_fusion = bf16[16,2,8,1024]{3,2,1,0:T(8,128)(2,1)} fusion(bf16[16,2,8,1024]{3,2,1,0:T(8,128)(2,1)} %bitcast.108, pred[16,2]{1,0:T(8,128)(4,1)S(1)} %broadcast_in_dim.126), kind=kLoop, calls=%fused_computation.43 | loop fusion | flops 262144 | bytes 1048608 | tf_op jit(solution)/shard_map/jit(_where)/select_n | solution.py:103
  44.0 6.0 %all-to-all-start.1 = ((bf16[16,2,8,1024]{3,2,1,0:T(8,128)(2,1)}), bf16[16,2,8,1024]{3,2,1,0:T(8,128)(2,1)}, u32[]{:S(2)}, u32[]{:S(2)}) async-start(bf16[16,2,8,1024]{3,2,1,0:T(8,128)(2,1)} %broadcast_select_fusion), calls=%async_computation.1 | async-start | bytes 1048576 | tf_op jit(solution)/shard_map/all_to_all | solution.py:123
  50.0 1.5 %gather_fusion.1 = bf16[16,8,1024]{2,1,0:T(8,128)(2,1)S(1)} fusion(bf16[16,8,1024]{2,1,0:T(8,128)(2,1)} %all-to-all-done, s32[1024]{0:T(1024)S(1)} %pad_clamp_fusion.1), kind=kCustom, calls=%fused_computation.1 | custom fusion | bytes 524352 | tf_op jit(solution)/shard_map/gather | solution.py:126
  52.4 1.8 %pad.4.clone = bf16[256,1024]{0,1:T(8,128)(2,1)} pad(bf16[128,1024]{0,1:T(8,128)(2,1)} %copy.68, bf16[]{:T(256)} %constant.109.clone.1), padding=0_128x0_0 | pad | bytes 786434 | tf_op jit(solution)/shard_map/jit(_pad)/pad | solution.py:58
  54.2 12.6 %while.16 = (s32[]{:T(128)}, f32[4,8,256]{2,1,0:T(8,128)S(1)}, f32[4,8,256]{2,1,0:T(8,128)S(1)}, f32[4,8,256,128]{3,2,1,0:T(8,128)}, s32[]{:T(128)}, /*index=5*/...) while((s32[]{:T(128)}, f32[4,8,256]{2,1,0:T(8,128)S(1)}, ...), condition=%wide.region_7.8_spmd, body=%wide.region_4.7_spmd.sunk | while | flops 1103122688 | bytes 71304368 | solution.py:67
  54.9 1.1 %fusion.61 = (bf16[256,512]{0,1:T(8,128)(2,1)S(1)}, bf16[256,512]{0,1:T(8,128)(2,1)S(1)}) fusion(bf16[256,1024]{0,1:T(8,128)(2,1)} %get-tuple-element.252), kind=kLoop, calls=%fused_computation.72.clone.1 | loop fusion | bytes 1048576 | tf_op jit(solution)/shard_map/while/body/slice | solution.py:35
  56.0 2.1 %bitcast_reduce_fusion.2 = (f32[4,8,256]{2,1,0:T(8,128)S(1)}, f32[4,256,256,8]{2,1,3,0:T(8,128)S(1)}) fusion(pred[256]{0:T(512)(128)(4,1)S(1)} %fusion.60, bf16[256,4,128,1]{0,2,3,1:T(8,128)(2,1)S(1)} %bitcast.101, bf16[256,4,8,128]{3,0,2,1:T(8,128)(2,1)S(1)} %get-tuple-element.253), kind=kOutput, calls=%fused_computation.4.clone.1 | convolution fusion | flops 543154176 | bytes 10780928 | tf_op jit(solution)/shard_map/while/body/tkgd,skd->kgts/dot_general | solution.py:36
  58.1 2.3 %fusion.62 = f32[4,8,256]{2,1,0:T(8,128)S(1)} fusion(f32[4,256,256,8]{2,1,3,0:T(8,128)S(1)} %get-tuple-element.222, f32[4,8,256]{2,1,0:T(8,128)S(1)} %max.7, pred[256]{0:T(512)(128)(4,1)S(1)} %fusion.60), kind=kLoop, calls=%fused_computation.9.clone.1 | loop fusion | flops 10477568 | bytes 8454400 | tf_op jit(solution)/shard_map/while/body/reduce_sum | solution.py:43
  60.5 4.3 %multiply_add_fusion.5 = f32[4,8,256,128]{3,2,1,0:T(8,128)S(1)} fusion(f32[4,8,256,128]{3,2,1,0:T(8,128)S(1)} %copy-done.3, f32[4,8,256]{2,1,0:T(8,128)S(1)} %get-tuple-element.224, bf16[256,4,128,1]{0,2,3,1:T(8,128)(2,1)S(1)} %bitcast.105, f32[4,256,256,8]{2,1,3,0:T(8,128)S(1)} %get-tuple-element.222, f32[4,8,256]{2,1,0:T(8,128)S(1)} %max.7, ...), kind=kOutput, calls=%fused_computation.11.clone.1 | convolution fusion | flops 549453824 | bytes 17105152 | tf_op jit(solution)/shard_map/while/body/kgts,skd->kgtd/dot_general | solution.py:44
  64.8 2.0 %copy-done.4 = f32[4,8,256,128]{3,2,1,0:T(8,128)} copy-done((f32[4,8,256,128]{3,2,1,0:T(8,128)}, f32[4,8,256,128]{3,2,1,0:T(8,128)S(1)}, u32[]{:S(2)}) %copy-start.4) | copy-done | bytes 4194328 | tf_op jit(solution)/shard_map/while
  66.8 2.9 %fusion.28 = bf16[256,4,8,128]{3,0,2,1:T(8,128)(2,1)S(1)} fusion(f32[4,8,256,128]{3,2,1,0:T(8,128)} %get-tuple-element.108, f32[4,8,256]{2,1,0:T(8,128)S(1)} %get-tuple-element.109), kind=kLoop, calls=%fused_computation.42 | loop fusion | flops 2097152 | bytes 6324224 | tf_op jit(solution)/shard_map/convert_element_type | solution.py:85
  69.6 1.4 %copy.50 = bf16[256,4,8,128]{3,2,1,0:T(8,128)(2,1)S(1)} copy(bf16[256,4,8,128]{3,0,2,1:T(8,128)(2,1)S(1)} %fusion.28) | data formatting | bytes 4194304 | tf_op jit(solution)/shard_map/convert_element_type | solution.py:85
  71.0 2.3 %copy.71 = bf16[32,8,32,128]{3,1,2,0:T(8,128)(2,1)} copy(bf16[32,8,32,128]{3,2,1,0:T(8,128)(2,1)S(1)} %bitcast.104) | data formatting | bytes 4194304
  73.3 1.9 %copy.87 = bf16[32,8,1024]{2,1,0:T(8,128)(2,1)} copy(bf16[32,8,1024]{2,1,0:T(8,128)(2,1)} %bitcast.25) | data formatting | bytes 1048576
  (39 shorter events, 8.9 us)
Async XLA Ops:
  0.6 1.3 %copy-start = (bf16[64,8,1024]{2,1,0:T(8,128)(2,1)S(1)}, bf16[64,8,1024]{2,1,0:T(8,128)(2,1)}, u32[]{:S(2)}) copy-start(bf16[64,8,1024]{2,1,0:T(8,128)(2,1)} %param.11) | copy-start | bytes 3145732
  3.9 40.1 %all-to-all-start = ((bf16[16,8,1024]{2,1,0:T(8,128)(2,1)}), bf16[16,8,1024]{2,1,0:T(8,128)(2,1)}, u32[]{:S(2)}, u32[]{:S(2)}) async-start(bf16[16,8,1024]{2,1,0:T(8,128)(2,1)} %broadcast_select_fusion.1), calls=%async_computation | async-start | bytes 524288 | tf_op jit(solution)/shard_map/all_to_all | solution.py:124
  16.5 10.2 %copy-start.2 = (bf16[256,4096]{0,1:T(8,128)(2,1)}, bf16[256,4096]{0,1:T(8,128)(2,1)S(1)}, u32[]{:S(2)}) copy-start(bf16[256,4096]{0,1:T(8,128)(2,1)S(1)} %copy.42) | copy-start | bytes 6291460
  21.3 3.2 %copy-start.1 = (f32[4,256,256,8]{2,1,3,0:T(8,128)}, f32[4,256,256,8]{2,1,3,0:T(8,128)S(1)}, u32[]{:S(2)}) copy-start(f32[4,256,256,8]{2,1,3,0:T(8,128)S(1)} %get-tuple-element.163) | copy-start | bytes 25165828
  21.3 6.0 %copy-start.5 = (bf16[256,512]{1,0:T(8,128)(2,1)S(1)}, bf16[256,512]{1,0:T(8,128)(2,1)}, u32[]{:S(2)}) copy-start(bf16[256,512]{1,0:T(8,128)(2,1)} %get-tuple-element.158) | copy-start | bytes 786436
  27.4 7.0 %copy-start.6 = (s32[16]{0:T(128)S(1)}, s32[16]{0:T(128)}, u32[]{:S(2)}) copy-start(s32[16]{0:T(128)} %param.14) | copy-start | bytes 196
  44.0 29.2 %all-to-all-start.1 = ((bf16[16,2,8,1024]{3,2,1,0:T(8,128)(2,1)}), bf16[16,2,8,1024]{3,2,1,0:T(8,128)(2,1)}, u32[]{:S(2)}, u32[]{:S(2)}) async-start(bf16[16,2,8,1024]{3,2,1,0:T(8,128)(2,1)} %broadcast_select_fusion), calls=%async_computation.1 | async-start | bytes 1048576 | tf_op jit(solution)/shard_map/all_to_all | solution.py:123
  56.0 4.5 %copy-start.3 = (f32[4,8,256,128]{3,2,1,0:T(8,128)S(1)}, f32[4,8,256,128]{3,2,1,0:T(8,128)}, u32[]{:S(2)}) copy-start(f32[4,8,256,128]{3,2,1,0:T(8,128)} %get-tuple-element.239) | copy-start | bytes 12582916 | tf_op jit(solution)/shard_map/while
  64.8 2.0 %copy-start.4 = (f32[4,8,256,128]{3,2,1,0:T(8,128)}, f32[4,8,256,128]{3,2,1,0:T(8,128)S(1)}, u32[]{:S(2)}) copy-start(f32[4,8,256,128]{3,2,1,0:T(8,128)S(1)} %multiply_add_fusion.5) | copy-start | bytes 12582916 | tf_op jit(solution)/shard_map/while
where the time goes:
time: 76 us; the launch traced here: 75.2 us
  local copies, waits for them, and re-layouts  29.7 us (39%)
  other arithmetic  15.5 us (20%)
  matrix products  14.9 us (20%)
  starting transfers between devices  13.4 us (18%)
  between operations  1.56 us (2%)
    unnamed x16, local copies, waits for them, and re-layouts  13 us
    dot_general x2, matrix products, absorb_block(): jnp.einsum('kgts,skd->kgtd', weights.astype(jnp.bfloat16), value_rows, pr...  11.3 us
    all_to_all x1, starting transfers between devices, on_device(): lax.all_to_all(prefix_out, 'pool', split_axis=0, concat_axis=0, tiled=True)  7.44 us
    all_to_all x1, starting transfers between devices, on_device(): lax.all_to_all(outbox, 'pool', split_axis=0, concat_axis=0, tiled=True)  6 us
    reduce_sum x2, other arithmetic, absorb_block(): run_total = factor * run_total + jnp.sum(weights, axis=-1)  4.43 us
    dot_general x2, matrix products, absorb_block(): jnp.einsum('tkgd,skd->kgts', query_groups, key_rows, preferred_element_ty...  3.59 us
    slice x2, local copies, waits for them, and re-layouts, absorb_block(): value_rows = kv_block[:, width_keys:].reshape(key_count, kv_heads, head_dim)  3.29 us
    while x1, local copies, waits for them, and re-layouts, attend_pages(): return lax.fori_loop(0, block_count, one_block, running)  3.05 us
  transfers between devices with their start and end apart: 2, of which 0 were waited for; matrix products, arithmetic and copies ran while one was open for 66% of the time, Pallas kernels for 0%

commit v1 on v0

v1 whole, which is shorter than its diff:
```python
import functools
import math

import jax
import jax.numpy as jnp
from jax import lax
from jax.experimental import pallas as pl
from jax.experimental.pallas import tpu as pltpu
from jax.sharding import PartitionSpec as P

HD = 128
PAGE = 8
KVH = 4
MASKED = -1e30
MESH = pl.DeviceIdType.MESH


def dot(a, b):
    return jnp.dot(a, b, preferred_element_type=jnp.float32)


def dot_t(a, b):
    return lax.dot_general(a, b, (((1,), (1,)), ((), ())), preferred_element_type=jnp.float32)


def iota(shape, dim):
    return lax.broadcasted_iota(jnp.int32, shape, dim)


def kernel(
    n, slots,
    q_hbm, kv_hbm, store_hbm, owner_ref, slot_ref, pages_ref, dest_ref,
    attn_hbm, inbox_hbm,
    q_ref, keys_ref, store_ref, pout_ref, arrived_ref, outbox_ref, bias_ref, attn_ref,
    in_sem, attn_sem, own_sem, psend, precv, isend, irecv,
):
    me = lax.axis_index("pool")
    tokens, width = q_ref.shape
    prefix = n * PAGE
    half = tokens // 2
    group = width // HD // KVH
    new_pages = dest_ref.shape[1]
    kv_width = keys_ref.shape[1]

    load_store = pltpu.make_async_copy(store_hbm, store_ref, in_sem.at[0])
    load_kv = pltpu.make_async_copy(kv_hbm, keys_ref.at[pl.ds(prefix, tokens)], in_sem.at[1])
    load_q = pltpu.make_async_copy(q_hbm, q_ref, in_sem.at[2])
    load_store.start()
    load_kv.start()
    load_q.start()

    def partner(i):
        step = n // 2 + ((i + 1) // 2) * (1 - 2 * (i % 2))
        return (me + step) % n

    barrier = pltpu.get_barrier_semaphore()

    def greet(i, carry):
        pl.semaphore_signal(barrier, inc=1, device_id={"pool": partner(i)}, device_id_type=MESH)
        return carry

    lax.fori_loop(0, n - 1, greet, 0)

    owner = owner_ref[...]
    pages_row = jnp.broadcast_to(pages_ref[...], (n, n))
    row_id, col_id = iota((n, n), 0), iota((n, n), 1)
    pages_col = jnp.sum(jnp.where(row_id == col_id, pages_row, 0), axis=1, keepdims=True)
    wanted = (owner == me) & (col_id < pages_col)
    slot_of = jnp.sum(jnp.where(wanted, slot_ref[...] + 1, 0), axis=1, keepdims=True) - 1
    expand = (iota((prefix, n), 0) // PAGE == iota((prefix, n), 1)).astype(jnp.bfloat16)
    slot_tok = dot(expand, jnp.broadcast_to(slot_of, (n, HD)).astype(jnp.float32).astype(jnp.bfloat16))
    stored_rows = store_ref.shape[0] * PAGE
    row_of = slot_tok.astype(jnp.int32) * PAGE + iota((prefix, HD), 0) % PAGE
    pick = jnp.concatenate(
        [(row_of == iota((prefix, HD), 1) + b).astype(jnp.float32).astype(jnp.bfloat16) for b in range(0, stored_rows, HD)],
        axis=1,
    )
    load_store.wait()
    stored = store_ref[...].astype(jnp.float32).reshape(stored_rows, kv_width).astype(jnp.bfloat16)
    pout_ref[...] = dot(pick, stored).reshape(n, PAGE, kv_width).astype(jnp.bfloat16)

    pl.semaphore_wait(barrier, n - 1)

    def send_page(i, carry):
        to = partner(i)
        pltpu.make_async_remote_copy(
            pout_ref.at[to], arrived_ref.at[me], psend, precv, device_id={"pool": to}, device_id_type=MESH
        ).start()
        return carry

    lax.fori_loop(0, n - 1, send_page, 0)

    dest = jnp.broadcast_to(dest_ref[...], (new_pages, new_pages))
    first, second = iota(dest.shape, 0), iota(dest.shape, 1)
    dest_col = jnp.sum(jnp.where(first == second, dest, 0), axis=1, keepdims=True)
    rank = jnp.sum(jnp.where((dest_col == dest) & (first < second), 1, 0), axis=0, keepdims=True)
    place = (dest_ref[...] * slots + rank).astype(jnp.float32)
    widen = (iota((new_pages, tokens), 1) // PAGE == iota((new_pages, tokens), 0)).astype(jnp.bfloat16)
    place_tok = dot(jnp.broadcast_to(place, (PAGE, new_pages)).astype(jnp.bfloat16), widen)[:1].astype(jnp.int32)
    out_rows = n * slots * PAGE
    goal = place_tok * PAGE + iota((1, tokens), 1) % PAGE
    permute = (iota((out_rows, tokens), 0) == goal).astype(jnp.float32).astype(jnp.bfloat16)
    load_kv.wait()
    new_rows = keys_ref[pl.ds(prefix, tokens), :]
    outbox_ref[...] = dot(permute, new_rows).reshape(n * slots, PAGE, kv_width).astype(jnp.bfloat16)

    def send_new(i, carry):
        to = partner(i)
        pltpu.make_async_remote_copy(
            outbox_ref.at[pl.ds(to * slots, slots)],
            inbox_hbm.at[pl.ds(me * slots, slots)],
            isend, irecv, device_id={"pool": to}, device_id_type=MESH,
        ).start()
        return carry

    lax.fori_loop(0, n - 1, send_new, 0)
    own_copy = pltpu.make_async_copy(
        outbox_ref.at[pl.ds(me * slots, slots)], inbox_hbm.at[pl.ds(me * slots, slots)], own_sem
    )
    own_copy.start()
    arrived_ref[me] = pout_ref[me]

    my_owner = owner_ref[pl.ds(me, 1), :]
    lane = iota((1, n), 1)
    my_pages = jnp.sum(jnp.where(lane == me, pages_ref[...], 0), axis=1, keepdims=True)
    held = jnp.broadcast_to(jnp.where(lane < my_pages, my_owner, -1), (n, n)) == row_id
    valid = jnp.sum(jnp.where(held, 1.0, 0.0), axis=1, keepdims=True)
    valid_tok = dot(expand, jnp.broadcast_to(valid, (n, half)).astype(jnp.bfloat16))
    bias_ref[pl.ds(0, prefix), :] = jnp.where(valid_tok > 0.5, 0.0, MASKED).astype(jnp.bfloat16)
    diagonal = jnp.where(iota((half, half), 0) > iota((half, half), 1), MASKED, 0.0).astype(jnp.bfloat16)
    bias_ref[pl.ds(prefix, half), :] = diagonal
    bias_ref[pl.ds(prefix + half, half), :] = jnp.zeros((half, half), jnp.bfloat16)
    bias_ref[pl.ds(prefix + 2 * half, half), :] = diagonal

    load_q.wait()
    pltpu.make_async_copy(
        arrived_ref.at[pl.ds(0, n - 1)], arrived_ref.at[pl.ds(0, n - 1)], precv
    ).wait()
    keys_ref[pl.ds(0, prefix), :] = (
        arrived_ref[...].astype(jnp.float32).reshape(prefix, kv_width).astype(jnp.bfloat16)
    )

    stack = group if prefix <= 256 else 1
    scale = math.log2(math.e) / math.sqrt(HD)
    unit = (iota((half, half), 0) == iota((half, half), 1)).astype(jnp.float32).astype(jnp.bfloat16)

    def attend(step, carry):
        kv_head = step * stack // group
        key_cols = pl.ds(pl.multiple_of(kv_head * HD, HD), HD)
        value_cols = pl.ds(pl.multiple_of(kv_head * HD + KVH * HD, HD), HD)
        heads = [pl.ds(pl.multiple_of((step * stack + i) * HD, HD), HD) for i in range(stack)]
        for part in range(2):
            rows = pl.ds(part * half, half)
            count = prefix + (part + 1) * half
            keys = keys_ref[pl.ds(0, count), key_cols]
            values = keys_ref[pl.ds(0, count), value_cols]
            bias = bias_ref[pl.ds(0, count), :] if part == 0 else jnp.concatenate(
                [bias_ref[pl.ds(0, prefix), :], bias_ref[pl.ds(prefix + half, 2 * half), :]], axis=0
            )
            keyed = jnp.concatenate([keys, bias], axis=1)
            summed = jnp.concatenate([values, jnp.ones((count, HD), jnp.bfloat16)], axis=1)
            query = jnp.concatenate(
                [jnp.concatenate([q_ref[rows, cols], unit], axis=1) for cols in heads], axis=0
            )
            scores = dot_t(query, keyed)
            top = jnp.max(scores, axis=1, keepdims=True)
            weights = jnp.exp2((scores - top) * scale).astype(jnp.bfloat16)
            mixed = dot(weights, summed)
            result = (mixed[:, :HD] / mixed[:, HD:]).astype(jnp.bfloat16)
            for i, cols in enumerate(heads):
                attn_ref[rows, cols] = result[i * half:(i + 1) * half]
        done = pl.ds(pl.multiple_of(step * stack * HD, HD), stack * HD)
        pltpu.make_async_copy(attn_ref.at[:, done], attn_hbm.at[:, done], attn_sem.at[step]).start()
        return carry

    steps = KVH * group // stack
    lax.fori_loop(0, steps, attend, 0)

    def finish(step, carry):
        done = pl.ds(pl.multiple_of(step * stack * HD, HD), stack * HD)
        pltpu.make_async_copy(attn_ref.at[:, done], attn_hbm.at[:, done], attn_sem.at[step]).wait()
        return carry

    lax.fori_loop(0, steps, finish, 0)
    own_copy.wait()
    others = pl.ds(0, n - 1)
    pltpu.make_async_copy(pout_ref.at[others], pout_ref.at[others], psend).wait()
    placed = pl.ds(0, (n - 1) * slots)
    pltpu.make_async_copy(outbox_ref.at[placed], outbox_ref.at[placed], isend).wait()
    pltpu.make_async_copy(inbox_hbm.at[placed], inbox_hbm.at[placed], irecv).wait()


def on_device(n, queries, new_kv, prefix_store, page_owner, page_slot, prefix_pages, decode_dest):
    tokens, width = queries.shape
    kv_width = new_kv.shape[1]
    slots = max(1, -(-decode_dest.shape[1] // n))
    prefix = n * PAGE
    bf16 = jnp.bfloat16
    hbm = pl.BlockSpec(memory_space=pl.ANY)
    vmem = pl.BlockSpec(memory_space=pltpu.VMEM)
    return pl.pallas_call(
        functools.partial(kernel, n, slots),
        out_shape=(
            jax.ShapeDtypeStruct((tokens, width), bf16),
            jax.ShapeDtypeStruct((n * slots, PAGE, kv_width), bf16),
        ),
        in_specs=[hbm, hbm, hbm, vmem, vmem, vmem, vmem],
        out_specs=(hbm, hbm),
        scratch_shapes=[
            pltpu.VMEM((tokens, width), bf16),
            pltpu.VMEM((prefix + tokens, kv_width), bf16),
            pltpu.VMEM(prefix_store.shape, bf16),
            pltpu.VMEM((n, PAGE, kv_width), bf16),
            pltpu.VMEM((n, PAGE, kv_width), bf16),
            pltpu.VMEM((n * slots, PAGE, kv_width), bf16),
            pltpu.VMEM((prefix + 3 * (tokens // 2), tokens // 2), bf16),
            pltpu.VMEM((tokens, width), bf16),
            pltpu.SemaphoreType.DMA((3,)),
            pltpu.SemaphoreType.DMA((width // HD,)),
            pltpu.SemaphoreType.DMA,
            pltpu.SemaphoreType.DMA,
            pltpu.SemaphoreType.DMA,
            pltpu.SemaphoreType.DMA,
            pltpu.SemaphoreType.DMA,
        ],
        compiler_params=pltpu.CompilerParams(
            collective_id=0, has_side_effects=True, vmem_limit_bytes=48 * 1024 * 1024
        ),
    )(queries, new_kv, prefix_store, page_owner, page_slot, prefix_pages.reshape(1, n), decode_dest)


def solution(mesh):
    return jax.shard_map(
        functools.partial(on_device, mesh.shape["pool"]),
        mesh=mesh,
        in_specs=(
            P(("groups", "pool"), None),
            P(("groups", "pool"), None),
            P(("groups", "pool"), None, None),
            P("groups", None),
            P("groups", None),
            P("groups"),
            P(("groups", "pool"), None),
        ),
        out_specs=(P(("groups", "pool"), None), P(("groups", "pool"), None, None)),
        check_vma=False,
    )
```

time: 76 us -> 31.5 us (0.41)
  Pallas kernels: 0 us -> 23.5 us
  local copies, waits for them, and re-layouts: 29.7 us -> 7.08 us
  other arithmetic: 15.5 us -> 0 us
  matrix products: 14.9 us -> 0 us
  starting transfers between devices: 13.4 us -> 0 us
  between operations: 1.56 us -> 0.65 us
    pallas_call x0 -> x1, Pallas kernels: none -> 23.5 us  [on_device(): pl.pallas_call(functools.partial(kernel, n, slots), out_shape=(jax.ShapeD...]
    dot_general x4 -> x0, matrix products: 14.9 us -> none  [the longest x2 11.3 us: absorb_block(): jnp.einsum('kgts,skd->kgtd', weights.astype(jnp.bfloat16), value_rows, pr...]
    all_to_all x2 -> x0, starting transfers between devices: 13.4 us -> none  [the longest x1 7.44 us: on_device(): lax.all_to_all(prefix_out, 'pool', split_axis=0, concat_axis=0, tiled=True)]
    reduce_sum x5 -> x0, other arithmetic: 6.37 us -> none  [the longest x2 4.43 us: absorb_block(): run_total = factor * run_total + jnp.sum(weights, axis=-1)]
    unnamed x16 -> x14, local copies, waits for them, and re-layouts: 13 us -> 7.08 us
    while x6 -> x0, local copies, waits for them, and re-layouts: 5.02 us -> none  [the longest x1 3.05 us: attend_pages(): return lax.fori_loop(0, block_count, one_block, running)]
    gather x3 -> x0, local copies, waits for them, and re-layouts: 4.49 us -> none  [the longest x1 2.42 us: build_outbox(): page_data = new_kv.reshape(page_count, PAGE, kv_width)[source_page]]
    select_n x5 -> x0, other arithmetic: 3.44 us -> none  [the longest x1 1.94 us: build_outbox(): jnp.where(filled[:, None, None], page_data, jnp.zeros_like(page_data))]
  transfers between devices with their start and end apart: 2 -> 0, of which waited for: 0 -> 0; matrix products, arithmetic and copies ran while one was open for 66% -> 0% of each run, Pallas kernels for 0% -> 0%
where the time goes in v1:
time: 31.5 us; the launch traced here: 31.2 us
  Pallas kernels  23.5 us (75%)
  local copies, waits for them, and re-layouts  7.08 us (22%)
  between operations  0.65 us (2%)
    pallas_call x1, Pallas kernels, on_device(): pl.pallas_call(functools.partial(kernel, n, slots), out_shape=(jax.ShapeD...  23.5 us
    unnamed x14, local copies, waits for them, and re-layouts  7.08 us

profile of v1, /device:TPU:0, one launch (start us, length us, event | category | flops | bytes accessed | tf_op | source)
XLA Modules:
  0.0 31.2 jit_solution(4909338043544548305)
XLA Ops:
  0.6 0.0 copy-start
  0.6 1.2 %copy-done = bf16[64,8,1024]{2,1,0:T(8,128)(2,1)S(1)} copy-done((bf16[64,8,1024]{2,1,0:T(8,128)(2,1)S(1)}, bf16[64,8,1024]{2,1,0:T(8,128)(2,1)}, u32[]{:S(2)}) %copy-start) | copy-done | bytes 1048600
  1.9 0.0 copy-start.1
  1.9 1.0 %copy-done.1 = bf16[256,1024]{1,0:T(8,128)(2,1)S(1)} copy-done((bf16[256,1024]{1,0:T(8,128)(2,1)S(1)}, bf16[256,1024]{1,0:T(8,128)(2,1)}, u32[]{:S(2)}) %copy-start.1) | copy-done | bytes 524312
  2.9 0.0 copy-start.2
  2.9 0.7 %copy-done.2 = s32[16,16]{1,0:T(8,128)S(1)} copy-done((s32[16,16]{1,0:T(8,128)S(1)}, s32[16,16]{1,0:T(8,128)}, u32[]{:S(2)}) %copy-start.2) | copy-done | bytes 1048
  3.6 0.0 copy-start.3
  3.6 0.7 %copy-done.3 = s32[16,16]{1,0:T(8,128)S(1)} copy-done((s32[16,16]{1,0:T(8,128)S(1)}, s32[16,16]{1,0:T(8,128)}, u32[]{:S(2)}) %copy-start.3) | copy-done | bytes 1048
  4.3 0.0 copy-start.4
  4.3 0.7 %copy-done.4 = s32[16]{0:T(128)S(1)} copy-done((s32[16]{0:T(128)S(1)}, s32[16]{0:T(128)}, u32[]{:S(2)}) %copy-start.4) | copy-done | bytes 88
  5.0 0.0 copy-start.5
  5.0 0.7 %copy-done.5 = s32[1,32]{1,0:T(1,128)S(1)} copy-done((s32[1,32]{1,0:T(1,128)S(1)}, s32[1,32]{1,0:T(1,128)}, u32[]{:S(2)}) %copy-start.5) | copy-done | bytes 152
  5.6 23.5 %shard_map.86 = (bf16[256,4096]{1,0:T(8,128)(2,1)S(1)}, bf16[32,8,1024]{2,1,0:T(8,128)(2,1)S(1)}) custom-call(bf16[256,4096]{1,0:T(8,128)(2,1)} %q_hbm.1, bf16[256,1024]{1,0:T(8,128)(2,1)S(1)} %copy-done.1, bf16[64,8,1024]{2,1,0:T(8,128)(2,1)S(1)} %copy-done, s32[16,16]{1,0:T(8,128)S(1)} %copy-done.2, s32[16,16]{1,0:T(8,128)S(1)} %copy-done.3, ...), custom_call_target="tpu_custom_call" | custom-call | tf_op jit(solution)/shard_map/pallas_call | solution.py:201
  29.1 1.3 %copy.11 = bf16[256,4096]{1,0:T(8,128)(2,1)} copy(bf16[256,4096]{1,0:T(8,128)(2,1)S(1)} %get-tuple-element.4) | data formatting | bytes 4194304
  30.4 0.8 %copy.12 = bf16[32,8,1024]{2,1,0:T(8,128)(2,1)} copy(bf16[32,8,1024]{2,1,0:T(8,128)(2,1)S(1)} %get-tuple-element.5) | data formatting | bytes 1048576
Async XLA Ops:
  0.6 1.2 %copy-start = (bf16[64,8,1024]{2,1,0:T(8,128)(2,1)S(1)}, bf16[64,8,1024]{2,1,0:T(8,128)(2,1)}, u32[]{:S(2)}) copy-start(bf16[64,8,1024]{2,1,0:T(8,128)(2,1)} %store_hbm.1) | copy-start | bytes 3145732
  1.9 1.0 %copy-start.1 = (bf16[256,1024]{1,0:T(8,128)(2,1)S(1)}, bf16[256,1024]{1,0:T(8,128)(2,1)}, u32[]{:S(2)}) copy-start(bf16[256,1024]{1,0:T(8,128)(2,1)} %kv_hbm.1) | copy-start | bytes 1572868
  2.9 0.7 %copy-start.2 = (s32[16,16]{1,0:T(8,128)S(1)}, s32[16,16]{1,0:T(8,128)}, u32[]{:S(2)}) copy-start(s32[16,16]{1,0:T(8,128)} %owner_ref.1) | copy-start | bytes 3076
  3.6 0.7 %copy-start.3 = (s32[16,16]{1,0:T(8,128)S(1)}, s32[16,16]{1,0:T(8,128)}, u32[]{:S(2)}) copy-start(s32[16,16]{1,0:T(8,128)} %slot_ref.1) | copy-start | bytes 3076
  4.3 0.7 %copy-start.4 = (s32[16]{0:T(128)S(1)}, s32[16]{0:T(128)}, u32[]{:S(2)}) copy-start(s32[16]{0:T(128)} %param.12) | copy-start | bytes 196
  5.0 0.7 %copy-start.5 = (s32[1,32]{1,0:T(1,128)S(1)}, s32[1,32]{1,0:T(1,128)}, u32[]{:S(2)}) copy-start(s32[1,32]{1,0:T(1,128)} %dest_ref.1) | copy-start | bytes 388

commit v2 on v1

--- a/solution.py
+++ b/solution.py
@@ -12,6 +12,8 @@
 PAGE = 8
 KVH = 4
 MASKED = -1e30
+CHUNKS = 4
+VMEM_BYTES = 64 * 1024 * 1024
 MESH = pl.DeviceIdType.MESH
 
 
@@ -29,9 +31,10 @@
 
 def kernel(
     n, slots,
-    q_hbm, kv_hbm, store_hbm, owner_ref, slot_ref, pages_ref, dest_ref,
+    q_hbm, kv_hbm, store_hbm, owner_hbm, slot_hbm, pages_hbm, dest_hbm,
     attn_hbm, inbox_hbm,
-    q_ref, keys_ref, store_ref, pout_ref, arrived_ref, outbox_ref, bias_ref, attn_ref,
+    attn_ref, q_ref, keys_ref, store_ref, owner_ref, slot_ref, pages_ref, dest_ref,
+    pout_ref, arrived_ref, outbox_ref, bias_ref,
     in_sem, attn_sem, own_sem, psend, precv, isend, irecv,
 ):
     me = lax.axis_index("pool")
@@ -45,6 +48,14 @@
     load_store = pltpu.make_async_copy(store_hbm, store_ref, in_sem.at[0])
     load_kv = pltpu.make_async_copy(kv_hbm, keys_ref.at[pl.ds(prefix, tokens)], in_sem.at[1])
     load_q = pltpu.make_async_copy(q_hbm, q_ref, in_sem.at[2])
+    tables = [
+        pltpu.make_async_copy(src, dst, in_sem.at[3 + i])
+        for i, (src, dst) in enumerate(
+            [(owner_hbm, owner_ref), (slot_hbm, slot_ref), (pages_hbm, pages_ref), (dest_hbm, dest_ref)]
+        )
+    ]
+    for load in tables:
+        load.start()
     load_store.start()
     load_kv.start()
     load_q.start()
@@ -60,6 +71,9 @@
         return carry
 
     lax.fori_loop(0, n - 1, greet, 0)
+
+    for load in tables:
+        load.wait()
 
     owner = owner_ref[...]
     pages_row = jnp.broadcast_to(pages_ref[...], (n, n))
@@ -143,6 +157,10 @@
     stack = group if prefix <= 256 else 1
     scale = math.log2(math.e) / math.sqrt(HD)
     unit = (iota((half, half), 0) == iota((half, half), 1)).astype(jnp.float32).astype(jnp.bfloat16)
+
+    def deliver(step):
+        done = pl.ds(pl.multiple_of(step * stack * HD, HD), stack * HD)
+        return pltpu.make_async_copy(attn_ref.at[:, done], attn_hbm.at[:, done], attn_sem.at[step])
 
     def attend(step, carry):
         kv_head = step * stack // group
@@ -169,16 +187,14 @@
             result = (mixed[:, :HD] / mixed[:, HD:]).astype(jnp.bfloat16)
             for i, cols in enumerate(heads):
                 attn_ref[rows, cols] = result[i * half:(i + 1) * half]
-        done = pl.ds(pl.multiple_of(step * stack * HD, HD), stack * HD)
-        pltpu.make_async_copy(attn_ref.at[:, done], attn_hbm.at[:, done], attn_sem.at[step]).start()
+        deliver(step).start()
         return carry
 
     steps = KVH * group // stack
     lax.fori_loop(0, steps, attend, 0)
 
     def finish(step, carry):
-        done = pl.ds(pl.multiple_of(step * stack * HD, HD), stack * HD)
-        pltpu.make_async_copy(attn_ref.at[:, done], attn_hbm.at[:, done], attn_sem.at[step]).wait()
+        deliver(step).wait()
         return carry
 
     lax.fori_loop(0, steps, finish, 0)
@@ -190,32 +206,54 @@
     pltpu.make_async_copy(inbox_hbm.at[placed], inbox_hbm.at[placed], irecv).wait()
 
 
+def hand_out(attn_in, inbox_in, attn_out, inbox_out, attn_ref, inbox_ref, sem):
+    into, out = [], []
+    for a, (source, held, target) in enumerate([(attn_in, attn_ref, attn_out), (inbox_in, inbox_ref, inbox_out)]):
+        rows = source.shape[0] // CHUNKS
+        for i in range(CHUNKS):
+            block = pl.ds(i * rows, rows)
+            into.append(pltpu.make_async_copy(source.at[block], held.at[block], sem.at[0, a * CHUNKS + i]))
+            out.append(pltpu.make_async_copy(held.at[block], target.at[block], sem.at[1, a * CHUNKS + i]))
+    for copy in into:
+        copy.start()
+    for arrived, leaving in zip(into, out):
+        arrived.wait()
+        leaving.start()
+    for copy in out:
+        copy.wait()
+
+
 def on_device(n, queries, new_kv, prefix_store, page_owner, page_slot, prefix_pages, decode_dest):
     tokens, width = queries.shape
     kv_width = new_kv.shape[1]
     slots = max(1, -(-decode_dest.shape[1] // n))
     prefix = n * PAGE
     bf16 = jnp.bfloat16
-    hbm = pl.BlockSpec(memory_space=pl.ANY)
+    hbm = pl.BlockSpec(memory_space=pltpu.HBM)
+    anywhere = pl.BlockSpec(memory_space=pl.ANY)
     vmem = pl.BlockSpec(memory_space=pltpu.VMEM)
-    return pl.pallas_call(
+    attention, inbox = pl.pallas_call(
         functools.partial(kernel, n, slots),
         out_shape=(
             jax.ShapeDtypeStruct((tokens, width), bf16),
             jax.ShapeDtypeStruct((n * slots, PAGE, kv_width), bf16),
         ),
-        in_specs=[hbm, hbm, hbm, vmem, vmem, vmem, vmem],
-        out_specs=(hbm, hbm),
+        in_specs=[hbm] * 7,
+        out_specs=(anywhere, anywhere),
         scratch_shapes=[
+            pltpu.VMEM((tokens, width), bf16),
             pltpu.VMEM((tokens, width), bf16),
             pltpu.VMEM((prefix + tokens, kv_width), bf16),
             pltpu.VMEM(prefix_store.shape, bf16),
+            pltpu.VMEM(page_owner.shape, jnp.int32),
+            pltpu.VMEM(page_slot.shape, jnp.int32),
+            pltpu.VMEM((1, n), jnp.int32),
+            pltpu.VMEM(decode_dest.shape, jnp.int32),
             pltpu.VMEM((n, PAGE, kv_width), bf16),
             pltpu.VMEM((n, PAGE, kv_width), bf16),
             pltpu.VMEM((n * slots, PAGE, kv_width), bf16),
             pltpu.VMEM((prefix + 3 * (tokens // 2), tokens // 2), bf16),
-            pltpu.VMEM((tokens, width), bf16),
-            pltpu.SemaphoreType.DMA((3,)),
+            pltpu.SemaphoreType.DMA((7,)),
             pltpu.SemaphoreType.DMA((width // HD,)),
             pltpu.SemaphoreType.DMA,
             pltpu.SemaphoreType.DMA,
@@ -224,9 +262,24 @@
             pltpu.SemaphoreType.DMA,
         ],
         compiler_params=pltpu.CompilerParams(
-            collective_id=0, has_side_effects=True, vmem_limit_bytes=48 * 1024 * 1024
+            collective_id=0, has_side_effects=True, vmem_limit_bytes=VMEM_BYTES
         ),
     )(queries, new_kv, prefix_store, page_owner, page_slot, prefix_pages.reshape(1, n), decode_dest)
+    return pl.pallas_call(
+        hand_out,
+        out_shape=(
+            jax.ShapeDtypeStruct(attention.shape, bf16),
+            jax.ShapeDtypeStruct(inbox.shape, bf16),
+        ),
+        in_specs=[hbm] * 2,
+        out_specs=(hbm, hbm),
+        scratch_shapes=[
+            pltpu.VMEM(attention.shape, bf16),
+            pltpu.VMEM(inbox.shape, bf16),
+            pltpu.SemaphoreType.DMA((2, 2 * CHUNKS)),
+        ],
+        compiler_params=pltpu.CompilerParams(vmem_limit_bytes=VMEM_BYTES),
+    )(attention, inbox)
 
 
 def solution(mesh):

time: 31.5 us -> 27.3 us (0.87)
  the two profiles are of different devices: /device:TPU:0 before, /device:TPU:13 now
where the time goes in v2:
time: 27.3 us; the launch traced here: 27.1 us
  Pallas kernels  26.4 us (97%)
  between operations  0.64 us (2%)
    pallas_call x1, Pallas kernels, on_device(): pl.pallas_call(functools.partial(kernel, n, slots), out_shape=(jax.ShapeD...  23.8 us
    pallas_call x1, Pallas kernels, on_device(): pl.pallas_call(hand_out, out_shape=(jax.ShapeDtypeStruct(attention.shape,...  2.66 us

profile of v2, /device:TPU:13, one launch (start us, length us, event | category | flops | bytes accessed | tf_op | source)
XLA Modules:
  0.0 27.1 jit_solution(863399997884364939)
XLA Ops:
  0.6 23.8 %shard_map.86 = (bf16[256,4096]{1,0:T(8,128)(2,1)}, bf16[32,8,1024]{2,1,0:T(8,128)(2,1)}) custom-call(bf16[256,4096]{1,0:T(8,128)(2,1)} %q_hbm.1, bf16[256,1024]{1,0:T(8,128)(2,1)} %kv_hbm.1, bf16[64,8,1024]{2,1,0:T(8,128)(2,1)} %store_hbm.1, s32[16,16]{1,0:T(8,128)} %owner_hbm.1, s32[16,16]{1,0:T(8,128)} %slot_hbm.1, s32[1,16]{1,0:T(1,128)} %bitcast.1, ...), custom_call_target="tpu_custom_call" | custom-call | tf_op jit(solution)/shard_map/pallas_call | solution.py:235
  24.4 2.7 %shard_map.87 = (bf16[256,4096]{1,0:T(8,128)(2,1)}, bf16[32,8,1024]{2,1,0:T(8,128)(2,1)}) custom-call(bf16[256,4096]{1,0:T(8,128)(2,1)} %get-tuple-element.4.attn_in, bf16[32,8,1024]{2,1,0:T(8,128)(2,1)} %get-tuple-element.5.inbox_in), custom_call_target="tpu_custom_call" | custom-call | tf_op jit(solution)/shard_map/pallas_call | solution.py:268

commit v3 on v2

--- a/solution.py
+++ b/solution.py
@@ -13,7 +13,7 @@
 KVH = 4
 MASKED = -1e30
 CHUNKS = 4
-VMEM_BYTES = 64 * 1024 * 1024
+VMEM_BYTES = 48 * 1024 * 1024
 MESH = pl.DeviceIdType.MESH
 
 
@@ -32,10 +32,10 @@
 def kernel(
     n, slots,
     q_hbm, kv_hbm, store_hbm, owner_hbm, slot_hbm, pages_hbm, dest_hbm,
-    attn_hbm, inbox_hbm,
-    attn_ref, q_ref, keys_ref, store_ref, owner_ref, slot_ref, pages_ref, dest_ref,
+    attn_ref, inbox_hbm,
+    q_ref, keys_ref, store_ref, owner_ref, slot_ref, pages_ref, dest_ref,
     pout_ref, arrived_ref, outbox_ref, bias_ref,
-    in_sem, attn_sem, own_sem, psend, precv, isend, irecv,
+    in_sem, own_sem, psend, precv, isend, irecv,
 ):
     me = lax.axis_index("pool")
     tokens, width = q_ref.shape
@@ -157,10 +157,6 @@
     stack = group if prefix <= 256 else 1
     scale = math.log2(math.e) / math.sqrt(HD)
     unit = (iota((half, half), 0) == iota((half, half), 1)).astype(jnp.float32).astype(jnp.bfloat16)
-
-    def deliver(step):
-        done = pl.ds(pl.multiple_of(step * stack * HD, HD), stack * HD)
-        return pltpu.make_async_copy(attn_ref.at[:, done], attn_hbm.at[:, done], attn_sem.at[step])
 
     def attend(step, carry):
         kv_head = step * stack // group
@@ -187,17 +183,11 @@
             result = (mixed[:, :HD] / mixed[:, HD:]).astype(jnp.bfloat16)
             for i, cols in enumerate(heads):
                 attn_ref[rows, cols] = result[i * half:(i + 1) * half]
-        deliver(step).start()
         return carry
 
     steps = KVH * group // stack
     lax.fori_loop(0, steps, attend, 0)
 
-    def finish(step, carry):
-        deliver(step).wait()
-        return carry
-
-    lax.fori_loop(0, steps, finish, 0)
     own_copy.wait()
     others = pl.ds(0, n - 1)
     pltpu.make_async_copy(pout_ref.at[others], pout_ref.at[others], psend).wait()
@@ -206,20 +196,15 @@
     pltpu.make_async_copy(inbox_hbm.at[placed], inbox_hbm.at[placed], irecv).wait()
 
 
-def hand_out(attn_in, inbox_in, attn_out, inbox_out, attn_ref, inbox_ref, sem):
-    into, out = [], []
-    for a, (source, held, target) in enumerate([(attn_in, attn_ref, attn_out), (inbox_in, inbox_ref, inbox_out)]):
-        rows = source.shape[0] // CHUNKS
-        for i in range(CHUNKS):
-            block = pl.ds(i * rows, rows)
-            into.append(pltpu.make_async_copy(source.at[block], held.at[block], sem.at[0, a * CHUNKS + i]))
-            out.append(pltpu.make_async_copy(held.at[block], target.at[block], sem.at[1, a * CHUNKS + i]))
-    for copy in into:
+def hand_out(attn_ref, inbox_ref, attn_hbm, inbox_hbm, sem):
+    rows = attn_ref.shape[0] // CHUNKS
+    copies = [
+        pltpu.make_async_copy(attn_ref.at[pl.ds(i * rows, rows)], attn_hbm.at[pl.ds(i * rows, rows)], sem.at[i])
+        for i in range(CHUNKS)
+    ] + [pltpu.make_async_copy(inbox_ref, inbox_hbm, sem.at[CHUNKS])]
+    for copy in copies:
         copy.start()
-    for arrived, leaving in zip(into, out):
-        arrived.wait()
-        leaving.start()
-    for copy in out:
+    for copy in copies:
         copy.wait()
 
 
@@ -230,18 +215,16 @@
     prefix = n * PAGE
     bf16 = jnp.bfloat16
     hbm = pl.BlockSpec(memory_space=pltpu.HBM)
-    anywhere = pl.BlockSpec(memory_space=pl.ANY)
     vmem = pl.BlockSpec(memory_space=pltpu.VMEM)
     attention, inbox = pl.pallas_call(
         functools.partial(kernel, n, slots),
         out_shape=(
-            jax.ShapeDtypeStruct((tokens, width), bf16),
-            jax.ShapeDtypeStruct((n * slots, PAGE, kv_width), bf16),
+            pltpu.VMEM((tokens, width), bf16),
+            pltpu.VMEM((n * slots, PAGE, kv_width), bf16),
         ),
         in_specs=[hbm] * 7,
-        out_specs=(anywhere, anywhere),
+        out_specs=(vmem, vmem),
         scratch_shapes=[
-            pltpu.VMEM((tokens, width), bf16),
             pltpu.VMEM((tokens, width), bf16),
             pltpu.VMEM((prefix + tokens, kv_width), bf16),
             pltpu.VMEM(prefix_store.shape, bf16),
@@ -254,7 +237,6 @@
             pltpu.VMEM((n * slots, PAGE, kv_width), bf16),
             pltpu.VMEM((prefix + 3 * (tokens // 2), tokens // 2), bf16),
             pltpu.SemaphoreType.DMA((7,)),
-            pltpu.SemaphoreType.DMA((width // HD,)),
             pltpu.SemaphoreType.DMA,
             pltpu.SemaphoreType.DMA,
             pltpu.SemaphoreType.DMA,
@@ -264,22 +246,20 @@
         compiler_params=pltpu.CompilerParams(
             collective_id=0, has_side_effects=True, vmem_limit_bytes=VMEM_BYTES
         ),
-    )(queries, new_kv, prefix_store, page_owner, page_slot, prefix_pages.reshape(1, n), decode_dest)
+    )(*[
+        pltpu.with_memory_space_constraint(x, pltpu.HBM)
+        for x in (queries, new_kv, prefix_store, page_owner, page_slot, prefix_pages.reshape(1, n), decode_dest)
+    ])
     return pl.pallas_call(
         hand_out,
         out_shape=(
             jax.ShapeDtypeStruct(attention.shape, bf16),
             jax.ShapeDtypeStruct(inbox.shape, bf16),
         ),
-        in_specs=[hbm] * 2,
+        in_specs=[vmem] * 2,
         out_specs=(hbm, hbm),
-        scratch_shapes=[
-            pltpu.VMEM(attention.shape, bf16),
-            pltpu.VMEM(inbox.shape, bf16),
-            pltpu.SemaphoreType.DMA((2, 2 * CHUNKS)),
-        ],
-        compiler_params=pltpu.CompilerParams(vmem_limit_bytes=VMEM_BYTES),
-    )(attention, inbox)
+        scratch_shapes=[pltpu.SemaphoreType.DMA((CHUNKS + 1,))],
+    )(*[pltpu.with_memory_space_constraint(x, pltpu.VMEM) for x in (attention, inbox)])
 
 
 def solution(mesh):

time: 27.3 us -> 25.4 us (0.930)
  the two profiles are of different devices: /device:TPU:13 before, /device:TPU:0 now
where the time goes in v3:
time: 25.4 us; the launch traced here: 25.2 us
  Pallas kernels  24.6 us (97%)
  between operations  0.64 us (3%)
    pallas_call x1, Pallas kernels, on_device(): pl.pallas_call(functools.partial(kernel, n, slots), out_shape=(pltpu.VMEM...  23 us
    pallas_call x1, Pallas kernels, on_device(): pl.pallas_call(hand_out, out_shape=(jax.ShapeDtypeStruct(attention.shape,...  1.53 us

profile of v3, /device:TPU:0, one launch (start us, length us, event | category | flops | bytes accessed | tf_op | source)
XLA Modules:
  0.0 25.2 jit_solution(7474119472685174214)
XLA Ops:
  0.6 23.0 %shard_map.86 = (bf16[256,4096]{1,0:T(8,128)(2,1)S(1)}, bf16[32,8,1024]{2,1,0:T(8,128)(2,1)S(1)}) custom-call(bf16[256,4096]{1,0:T(8,128)(2,1)} %q_hbm.1, bf16[256,1024]{1,0:T(8,128)(2,1)} %kv_hbm.1, bf16[64,8,1024]{2,1,0:T(8,128)(2,1)} %store_hbm.1, s32[16,16]{1,0:T(8,128)} %owner_hbm.1, s32[16,16]{1,0:T(8,128)} %slot_hbm.1, s32[1,16]{1,0:T(1,128)} %bitcast.1, ...), custom_call_target="tpu_custom_call" | custom-call | tf_op jit(solution)/shard_map/pallas_call | solution.py:219
  23.7 1.5 %shard_map.87 = (bf16[256,4096]{1,0:T(8,128)(2,1)}, bf16[32,8,1024]{2,1,0:T(8,128)(2,1)}) custom-call(bf16[256,4096]{1,0:T(8,128)(2,1)S(1)} %get-tuple-element.4.attn_ref, bf16[32,8,1024]{2,1,0:T(8,128)(2,1)S(1)} %get-tuple-element.5.inbox_ref), custom_call_target="tpu_custom_call" | custom-call | tf_op jit(solution)/shard_map/pallas_call | solution.py:253
